TPU v7x, 32 devices: a whole 2x2x4 slice. The times are simulated.
32 devices in a mesh: groups: 2 (over y), tensor: 4 (over z), expert: 4 (over x, core).
Axes of the slice: x: 2, y: 2, z: 4, core: 2. Of those that a mesh axis runs over, the one named last changes fastest.
Arguments:
- center: bfloat16 [32, 6144], P(('groups', 'expert')), parts along dimension 0, may hold values from -6 to 6
- gens: bfloat16 [32, 64, 6144], P(('groups', 'expert'), 'tensor'), parts along dimension 0, may hold values from -3 to 3
- query: bfloat16 [32, 6144], P(('groups', 'expert')), parts along dimension 0, may hold values from -6 to 6
- routes: int32 [32, 2], P(('groups', 'expert')), parts along dimension 0, may hold values from 0 to 3, as said below
- route_weights: float32 [32, 2], P(('groups', 'expert')), parts along dimension 0, may hold values from 0.25 to 1
- gate_weight: bfloat16 [4, 6144, 8192], P('expert', None, 'tensor'), may hold values from -0.078125 to 0.078125
- up_weight: bfloat16 [4, 6144, 8192], P('expert', None, 'tensor'), may hold values from -0.078125 to 0.078125
- down_weight: bfloat16 [4, 8192, 6144], P('expert', 'tensor'), may hold values from -0.0625 to 0.0625
- block_mask: int32 [4, 3, 48, 64], P('expert', None, None, 'tensor'), may hold values 0 or 1
Outputs:
- center_out: bfloat16 [32, 6144], P(('groups', 'expert')), parts along dimension 0
- gens_out: bfloat16 [32, 64, 6144], P(('groups', 'expert'), 'tensor'), parts along dimension 0
- radius: float32 [32, 6144], P(('groups', 'expert')), parts along dimension 0
- adjoint: float32 [32, 6144], P(('groups', 'expert')), parts along dimension 0
There are 2 independent parts, one for each index of `groups`. A program takes and returns all parts, laid end to end along the dimension named above; an argument that names none is the same for every part. Nothing has to cross between parts.
Inputs may be any that keep to these rules, and one draw needn't show every extreme that they name: `routes`: each token names two different experts. In every aligned block of 4 tokens (those of one index of expert), no expert is named by more than 3 tokens, and one expert, the same in all blocks of a draw, is named by exactly 3.
All inputs are finite; a program needn't handle non-finite values. No bound on the sum of `block_mask` on one device may be relied on, other than what follows from the above.
Results may differ from a plain program's by a relative error of at most 0.0075.
Values may be sent and summed in bfloat16 or wider, within the bound.
A program may use at most 512 MiB of HBM per device.

v0:
```python
import jax
import jax.numpy as jnp
from jax import lax
from jax.sharding import PartitionSpec as P

BLK = 128
MOST = 3


def shards(
    center, gens, query, routes, route_weights, gate_weight, up_weight, down_weight, block_mask
):
    experts = lax.axis_size("expert")
    slots = experts * MOST
    rows_here = gens.shape[1]
    width = gens.shape[2]
    hidden_here = gate_weight.shape[2]
    expert_ids = jnp.arange(experts, dtype=jnp.int32)
    named = (routes[:, :, None] == expert_ids[None, None, :]).astype(jnp.int32)
    per_token = jnp.sum(named, axis=1)
    earlier = jnp.cumsum(per_token, axis=0) - per_token
    slot_of = jnp.sum(named * earlier[:, None, :], axis=2)
    target = routes * MOST + slot_of
    slot_ids = jnp.arange(slots, dtype=jnp.int32)
    hits = (target[:, :, None] == slot_ids[None, None, :]).astype(jnp.float32)
    select = jnp.sum(hits, axis=1).astype(jnp.bfloat16)
    combine_weights = jnp.sum(hits * route_weights[:, :, None], axis=1)
    send_gens = jnp.einsum("bs,brd->srd", select, gens, preferred_element_type=jnp.float32).astype(
        jnp.bfloat16
    )
    pair_in = jnp.stack([center, query], axis=1)
    send_pair = jnp.einsum(
        "bs,brd->srd", select, pair_in, preferred_element_type=jnp.float32
    ).astype(jnp.bfloat16)
    recv_gens, recv_pair = (
        lax.all_to_all(
            send_gens.reshape(experts, MOST, rows_here, width),
            "expert",
            split_axis=0,
            concat_axis=0,
            tiled=True,
        ),
        lax.all_to_all(
            send_pair.reshape(experts, MOST, 2, width),
            "expert",
            split_axis=0,
            concat_axis=0,
            tiled=True,
        ),
    )
    recv_gens = recv_gens.reshape(slots, rows_here, width)
    recv_pair = recv_pair.reshape(slots, 2, width)
    mask_here = block_mask[0].astype(jnp.bfloat16)
    width_blocks = width // BLK
    hidden_blocks = hidden_here // BLK
    gate_masked = (
        gate_weight[0].reshape(width_blocks, BLK, hidden_blocks, BLK)
        * mask_here[0][:, None, :, None]
    ).reshape(width, hidden_here)
    up_masked = (
        up_weight[0].reshape(width_blocks, BLK, hidden_blocks, BLK) * mask_here[1][:, None, :, None]
    ).reshape(width, hidden_here)
    down_masked = (
        down_weight[0].reshape(hidden_blocks, BLK, width_blocks, BLK)
        * mask_here[2].T[:, None, :, None]
    ).reshape(hidden_here, width)
    both_in = jnp.concatenate([gate_masked, up_masked], axis=1)
    gen_pre = jnp.einsum(
        "srd,dh->srh",
        lax.all_gather(recv_gens, "tensor", axis=1, tiled=True),
        both_in,
        preferred_element_type=jnp.float32,
    )
    center_pre = jnp.dot(recv_pair[:, 0], both_in, preferred_element_type=jnp.float32)
    gate_center = center_pre[:, :hidden_here]
    up_center = center_pre[:, hidden_here:]
    sigma = 1.0 / (1.0 + jnp.exp(-gate_center))
    activated = gate_center * sigma
    slope_gate = sigma * (1.0 + gate_center * (1.0 - sigma)) * up_center
    hidden_center = (activated * up_center).astype(jnp.bfloat16)
    hidden_gens = (
        slope_gate[:, None, :] * gen_pre[:, :, :hidden_here]
        + activated[:, None, :] * gen_pre[:, :, hidden_here:]
    ).astype(jnp.bfloat16)
    out_center = jnp.dot(hidden_center, down_masked, preferred_element_type=jnp.float32)
    adjoint_hidden = jnp.einsum(
        "sd,hd->sh", recv_pair[:, 1], down_masked, preferred_element_type=jnp.float32
    )
    adjoint_pre = jnp.concatenate(
        [
            (adjoint_hidden * slope_gate).astype(jnp.bfloat16),
            (adjoint_hidden * activated).astype(jnp.bfloat16),
        ],
        axis=1,
    )
    adjoint_in = jnp.einsum("sh,dh->sd", adjoint_pre, both_in, preferred_element_type=jnp.float32)
    pair_out = jnp.stack([out_center, adjoint_in], axis=0)
    out_gens = jnp.einsum(
        "srh,hd->rsd", hidden_gens, down_masked, preferred_element_type=jnp.float32
    )
    all_rows = out_gens.shape[0]
    back_gens, back_pair = (
        lax.all_to_all(
            out_gens.reshape(all_rows, experts, MOST, width),
            "expert",
            split_axis=1,
            concat_axis=1,
            tiled=True,
        ),
        lax.all_to_all(
            pair_out.reshape(2, experts, MOST, width),
            "expert",
            split_axis=1,
            concat_axis=1,
            tiled=True,
        ),
    )
    gens_partial = jnp.einsum(
        "bs,rsd->brd",
        combine_weights,
        back_gens.reshape(all_rows, slots, width),
        precision=lax.Precision.HIGHEST,
    )
    pair_partial = jnp.einsum(
        "bs,rsd->rbd",
        combine_weights,
        back_pair.reshape(2, slots, width),
        precision=lax.Precision.HIGHEST,
    )
    token_gens = lax.psum_scatter(gens_partial, "tensor", scatter_dimension=1, tiled=True)
    token_pair = lax.psum(pair_partial, "tensor")
    radius_part = jnp.sum(jnp.abs(token_gens), axis=1)
    radius = lax.psum(radius_part.astype(jnp.bfloat16), "tensor").astype(jnp.float32)
    return (
        token_pair[0].astype(jnp.bfloat16),
        token_gens.astype(jnp.bfloat16),
        radius,
        token_pair[1],
    )


def solution(mesh):
    placed = (
        P(("groups", "expert"), None),
        P(("groups", "expert"), "tensor", None),
        P(("groups", "expert"), None),
        P(("groups", "expert"), None),
        P(("groups", "expert"), None),
        P("expert", None, "tensor"),
        P("expert", None, "tensor"),
        P("expert", "tensor", None),
        P("expert", None, None, "tensor"),
    )
    return jax.shard_map(
        shards,
        mesh=mesh,
        in_specs=placed,
        out_specs=(
            P(("groups", "expert"), None),
            P(("groups", "expert"), "tensor", None),
            P(("groups", "expert"), None),
            P(("groups", "expert"), None),
        ),
        check_vma=False,
    )
```

profile of v0, /device:TPU:0, one launch (start us, length us, event | category | flops | bytes accessed | tf_op | source)
XLA Modules:
  0.0 819.5 jit_solution(17590940010263337281)
XLA Ops:
  9.6 1.3 select_reduce_fusion
  11.0 1.4 convolution_convert_fusion
  12.4 2.7 copy.88
  15.1 4.2 all-to-all-start.2
  20.2 1.1 convolution_convert_fusion.1
  21.4 1.0 copy.80
  22.4 25.4 %all-to-all-done.2 = bf16[4,3,16,6144]{3,2,1,0:T(8,128)(2,1)S(1)} async-done(((bf16[4,3,16,6144]{3,2,1,0:T(8,128)(2,1)}), bf16[4,3,16,6144]{3,2,1,0:T(8,128)(2,1)S(1)}, u32[]{:S(2)}, u32[]{:S(2)}) %all-to-all-start.2) | async-done | bytes 2359328 | tf_op jit(solution)/shard_map/all_to_all | solution.py:36
  47.8 3.5 all-to-all-start
  52.0 4.3 mul.105
  56.3 9.4 %mul.109 = bf16[48,128,16,128]{3,2,1,0:T(8,128)(2,1)} broadcast(bf16[48,16]{1,0:T(8,128)(2,1)S(1)} %copy.82), dimensions={0,2} | broadcast | bytes 25167360 | tf_op jit(solution)/shard_map/mul | solution.py:61
  65.7 43.0 %bitcast_multiply_fusion.1 = (bf16[6144,2048]{1,0:T(8,128)(2,1)}, bf16[6144,2048]{1,0:T(8,128)(2,1)}) fusion(bf16[768,8,16,128]{3,2,1,0:T(8,128)(2,1)} %bitcast.94, bf16[1,6144,2048]{2,1,0:T(8,128)(2,1)} %param.15, bf16[768,8,16,128]{3,2,1,0:T(8,128)(2,1)S(1)} %bitcast.93, bf16[1,6144,2048]{2,1,0:T(8,128)(2,1)} %param.14), kind=kLoop, calls=%fused_computation.7 | loop fusion | flops 25165824 | bytes 150994944 | tf_op jit(solution)/shard_map/mul | solution.py:61
  108.7 8.9 %mul.114 = bf16[16,128,48,128]{3,2,1,0:T(8,128)(2,1)} broadcast(bf16[16,48]{1,0:T(8,128)(2,1)S(1)} %get-tuple-element.39), dimensions={0,2} | broadcast | bytes 25167360 | tf_op jit(solution)/shard_map/mul | solution.py:64
  117.6 35.5 %mul.115 = bf16[1,2048,6144]{2,1,0:T(8,128)(2,1)} reshape(bf16[16,128,48,128]{3,2,1,0:T(8,128)(2,1)} %mul.114) | data formatting | bytes 50331648 | tf_op jit(solution)/shard_map/mul | solution.py:64
  153.5 17.6 %fusion.14 = f32[12,4096]{1,0:T(8,128)S(1)} fusion(bf16[6144,2048]{1,0:T(8,128)(2,1)} %get-tuple-element.42, bf16[6144,2048]{1,0:T(8,128)(2,1)} %get-tuple-element.43, bf16[12,1,6144]{2,1,0:T(2,128)(2,1)S(1)} %get-tuple-element.35), kind=kOutput, calls=%fused_computation.17 | convolution fusion | flops 704643072 | bytes 50675712 | tf_op jit(solution)/shard_map/dot_general | solution.py:74
  171.1 18.1 %multiply_convert_fusion.1 = (bf16[12,2048]{1,0:T(8,128)(2,1)S(1)}, f32[12,2048]{1,0:T(8,128)S(1)}, bf16[12,2048]{1,0:T(8,128)(2,1)S(1)}, f32[12,2048]{1,0:T(8,128)S(1)}, bf16[12,2048]{1,0:T(8,128)(2,1)S(1)}) fusion(f32[12,4096]{1,0:T(8,128)S(1)} %fusion.14, bf16[1,2048,6144]{2,1,0:T(8,128)(2,1)} %param.16, bf16[1,2048,6144]{2,1,0:T(8,128)(2,1)} %mul.115, ...), kind=kOutput, calls=%fused_computation.43 | convolution fusion | flops 314941440 | bytes 51019776 | tf_op jit(solution)/shard_map/sd,hd->sh/dot_general | solution.py:86
  189.2 19.9 %fusion.13 = f32[12,6144]{1,0:T(8,128)S(1)} fusion(bf16[6144,2048]{1,0:T(8,128)(2,1)} %get-tuple-element.42, bf16[6144,2048]{1,0:T(8,128)(2,1)} %get-tuple-element.43, bf16[12,2048]{1,0:T(8,128)(2,1)S(1)} %get-tuple-element.34, bf16[12,2048]{1,0:T(8,128)(2,1)S(1)} %get-tuple-element.32), kind=kOutput, calls=%fused_computation.16 | convolution fusion | flops 704839680 | bytes 50724864 | tf_op jit(solution)/shard_map/sh,dh->sd/dot_general | solution.py:96
  209.5 16.8 %fusion.17 = f32[1,4,3,6144]{3,1,2,0:T(4,128)S(1)} fusion(bf16[1,2048,6144]{2,1,0:T(8,128)(2,1)} %param.16, bf16[1,2048,6144]{2,1,0:T(8,128)(2,1)} %mul.115, bf16[4,3,2048]{2,1,0:T(4,128)(2,1)S(1)} %reshape.80), kind=kOutput, calls=%fused_computation.22 | convolution fusion | flops 314572800 | bytes 50675712 | tf_op jit(solution)/shard_map/dot_general | solution.py:85
  226.5 1.3 copy.85
  227.7 3.7 all-to-all-start.1
  231.5 47.7 %fusion = f32[12,64,4096]{2,1,0:T(8,128)} fusion(bf16[12,64,6144]{2,1,0:T(8,128)(2,1)} %all-gather.2.cloned.1.call-done, bf16[6144,2048]{1,0:T(8,128)(2,1)} %get-tuple-element.42, bf16[6144,2048]{1,0:T(8,128)(2,1)} %get-tuple-element.43), kind=kOutput, calls=%fused_computation.1 | convolution fusion | flops 38755368960 | bytes 72351744 | tf_op jit(solution)/shard_map/srd,dh->srh/dot_general | solution.py:68
  279.1 32.4 %fusion.3 = f32[6144,12,64]{0,2,1:T(8,128)} fusion(bf16[256,8,48,128]{3,2,1,0:T(8,128)(2,1)} %bitcast.92, bf16[1,2048,6144]{2,1,0:T(8,128)(2,1)} %param.16, f32[12,64,4096]{2,1,0:T(8,128)} %fusion, f32[12,2048]{1,0:T(8,128)S(1)} %get-tuple-element.37, f32[12,2048]{1,0:T(8,128)S(1)} %get-tuple-element.33), kind=kOutput, calls=%fused_computation.5 | convolution fusion | flops 19383975936 | bytes 81985536 | tf_op jit(solution)/shard_map/srh,hd->rsd/dot_general | solution.py:98
  311.6 7.4 all-to-all-start.3
  319.3 1.7 convolution_bitcast_fusion
  321.1 203.5 %all-to-all-done.3 = f32[64,4,3,6144]{3,0,2,1:T(8,128)} async-done(((f32[64,4,3,6144]{3,0,2,1:T(8,128)}), f32[64,4,3,6144]{3,0,2,1:T(8,128)}, u32[]{:S(2)}, u32[]{:S(2)}) %all-to-all-start.3) | async-done | bytes 18874400 | tf_op jit(solution)/shard_map/all_to_all | solution.py:103
  524.5 31.7 %fusion.11 = f32[4,64,6144]{2,0,1:T(4,128)} fusion(f32[64,12,6144]{2,0,1:T(8,128)} %bitcast.25, f32[4,12]{1,0:T(4,128)S(1)} %copy-done.3), kind=kOutput, calls=%fused_computation.14 | convolution fusion | flops 226492416 | bytes 25166016 | tf_op jit(solution)/shard_map/bs,rsd->brd/dot_general | solution.py:118
  557.5 229.5 %all-reduce.4.cloned.1.call-done = (f32[2,4,6144]{2,1,0:T(4,128)}, f32[4,64,6144]{2,0,1:T(4,128)}) async-done(((f32[2,4,6144]{2,1,0:T(4,128)}, f32[4,64,6144]{2,0,1:T(4,128)}), (f32[2,4,6144]{2,1,0:T(4,128)}, f32[4,64,6144]{2,0,1:T(4,128)})) %all-reduce.4.cloned.1.call-update) | async-done | bytes 6488080 | tf_op jit(solution)/shard_map/psum | solution.py:131
  787.0 1.7 dynamic-slice_convert_fusion
  788.8 1.9 abs_reduce_fusion
  790.6 1.5 slice_bitcast_fusion
  792.2 1.5 fusion.38
  793.7 1.3 copy.90
  795.0 17.0 %psum.15 = bf16[4,6144]{1,0:T(4,128)(2,1)S(1)} all-reduce(bf16[4,6144]{1,0:T(4,128)(2,1)S(1)} %abs_reduce_fusion), channel_id=1, replica_groups=mesh['groups'=2,'tensor'=4,'expert'=4] {'tensor'}, use_global_device_ids=true, to_apply=%region_8.9 | all-reduce | flops 24576 | bytes 98304 | tf_op jit(solution)/shard_map/psum | solution.py:133
  (33 shorter events, 6.7 us)
Async XLA Ops:
  7.2 3.8 copy-start
  15.1 32.7 %all-to-all-start.2 = ((bf16[4,3,16,6144]{3,2,1,0:T(8,128)(2,1)}), bf16[4,3,16,6144]{3,2,1,0:T(8,128)(2,1)S(1)}, u32[]{:S(2)}, u32[]{:S(2)}) async-start(bf16[4,3,16,6144]{3,2,1,0:T(8,128)(2,1)} %bitcast.97), calls=%async_computation.2 | async-start | bytes 4718592 | tf_op jit(solution)/shard_map/all_to_all | solution.py:36
  47.8 3.7 copy-start.2
  47.8 105.3 %all-to-all-start = ((bf16[4,3,2,6144]{3,2,1,0:T(2,128)(2,1)}), bf16[4,3,2,6144]{3,2,1,0:T(2,128)(2,1)S(1)}, u32[]{:S(2)}, u32[]{:S(2)}) async-start(bf16[4,3,2,6144]{3,2,1,0:T(2,128)(2,1)} %bitcast.3), calls=%async_computation | async-start | bytes 589824 | tf_op jit(solution)/shard_map/all_to_all | solution.py:43
  51.3 180.2 %all-gather.2.cloned.1.call-start = ((), (), s32[]{:S(2)}) async-start(), calls=%async_computation.4 | async-start | bytes 11796480 | tf_op jit(solution)/shard_map/all_gather | solution.py:70
  227.7 83.9 %all-to-all-start.1 = ((f32[2,4,3,6144]{3,0,2,1:T(2,128)}), f32[2,4,3,6144]{3,0,2,1:T(2,128)S(1)}, u32[]{:S(2)}, u32[]{:S(2)}) async-start(f32[2,4,3,6144]{3,0,2,1:T(2,128)} %copy.85), calls=%async_computation.1 | async-start | bytes 1179648 | tf_op jit(solution)/shard_map/all_to_all | solution.py:110
  311.6 7.7 copy-start.3
  311.6 212.9 %all-to-all-start.3 = ((f32[64,4,3,6144]{3,0,2,1:T(8,128)}), f32[64,4,3,6144]{3,0,2,1:T(8,128)}, u32[]{:S(2)}, u32[]{:S(2)}) async-start(f32[64,4,3,6144]{3,0,2,1:T(8,128)} %bitcast.95), calls=%async_computation.3 | async-start | bytes 37748736 | tf_op jit(solution)/shard_map/all_to_all | solution.py:103
  319.0 237.3 %copy-start.4 = (u32[32]{0:T(128)S(1)}, u32[32]{0:T(128)}, u32[]{:S(2)}) copy-start(u32[32]{0:T(128)} %constant.24) | copy-start | bytes 388
  319.0 493.7 %copy-start.1 = (bf16[4,16,6144]{2,1,0:T(8,128)(2,1)S(1)}, bf16[4,16,6144]{2,1,0:T(8,128)(2,1)}, u32[]{:S(2)}) copy-start(bf16[4,16,6144]{2,1,0:T(8,128)(2,1)} %param.10) | copy-start | bytes 2359300
  319.0 468.0 %all-reduce.4.cloned.1.call-start = ((), (), s32[]{:S(2)}) async-start(), calls=%async_computation.5 | async-start | bytes 12976128 | tf_op jit(solution)/shard_map/psum | solution.py:131
Sparse Core Ops, SparseCore 0:
  53.7 169.3 all-gather.1
  556.4 230.6 all-reduce.3
where the time goes:
time: 821 us; the launch traced here: 820 us
  waiting for transfers between devices  459 us (56%)
  matrix products  188 us (23%)
  local copies, waits for them, and re-layouts  70.8 us (9%)
  other arithmetic  50.2 us (6%)
  starting transfers between devices  19.3 us (2%)
  blocking collectives  17 us (2%)
  between operations  14.9 us (2%)
    psum x1, waiting for transfers between devices, shards(): token_pair = lax.psum(pair_partial, 'tensor')  230 us
    all_to_all x1, waiting for transfers between devices, shards(): lax.all_to_all(out_gens.reshape(all_rows, experts, MOST, width), 'expert'...  203 us
    dot_general x1, matrix products, shards(): jnp.einsum('srd,dh->srh', lax.all_gather(recv_gens, 'tensor', axis=1, til...  47.7 us
    mul x2, local copies, waits for them, and re-layouts, shards(): down_weight[0].reshape(hidden_blocks, BLK, width_blocks, BLK)  44.4 us
    mul x1, other arithmetic, shards(): up_weight[0].reshape(width_blocks, BLK, hidden_blocks, BLK)  43 us
    dot_general x1, matrix products, shards(): jnp.einsum('srh,hd->rsd', hidden_gens, down_masked, preferred_element_typ...  32.4 us
    dot_general x1, matrix products, shards(): jnp.einsum('bs,rsd->brd', combine_weights, back_gens.reshape(all_rows, sl...  31.7 us
    all_to_all x1, waiting for transfers between devices, shards(): lax.all_to_all(send_gens.reshape(experts, MOST, rows_here, width), 'exper...  25.4 us
  transfers between devices with their start and end apart: 6, of which 3 were waited for; matrix products, arithmetic and copies ran while one was open for 32% of the time, Pallas kernels for 0%

commit v1 on v0

v1 whole, which is shorter than its diff:
```python
import functools

import jax
import jax.numpy as jnp
from jax import lax
from jax.experimental import pallas as pl
from jax.experimental.pallas import tpu as pltpu
from jax.sharding import PartitionSpec as P

BLK = 128
MOST = 3
CHUNKS_IN = 3
CHUNKS_OUT = 4
COST_SHARE = 20
VMEM = 56 * 2**20
F32 = jnp.float32
BF16 = jnp.bfloat16


def params():
    return pltpu.CompilerParams(vmem_limit_bytes=VMEM)


def cost(flops, nbytes):
    return pl.CostEstimate(
        flops=flops // COST_SHARE, bytes_accessed=nbytes // COST_SHARE, transcendentals=0
    )


def after(value, *others):
    return lax.optimization_barrier((value, *others))[0]


def mask_in_kernel(gate_ref, up_ref, gate_mask, up_mask, center_ref, *refs):
    gate_out, up_out, gc_ref, uc_ref = refs[-4:]
    for k in range(gate_ref.shape[0] // BLK):
        rows = slice(k * BLK, (k + 1) * BLK)
        gate_out[rows, :] = gate_ref[rows, :] * gate_mask[k : k + 1, :]
        up_out[rows, :] = up_ref[rows, :] * up_mask[k : k + 1, :]
    center = center_ref[...]
    gc_ref[...] = jnp.dot(center, gate_out[...], preferred_element_type=F32)
    uc_ref[...] = jnp.dot(center, up_out[...], preferred_element_type=F32)


def mask_in(gate, up, gate_mask, up_mask, center, part, parts, before):
    width, hidden = gate.shape
    tokens = center.shape[0]
    tile = min(256, hidden // parts)
    steps = hidden // parts // tile
    start = part * steps
    weight = pl.BlockSpec((width, tile), lambda n: (0, start + n))
    mask = pl.BlockSpec((width // BLK, tile), lambda n: (0, start + n))
    pre = pl.BlockSpec((tokens, tile), lambda n: (0, n))
    return pl.pallas_call(
        mask_in_kernel,
        grid=(steps,),
        in_specs=[weight, weight, mask, mask, pl.BlockSpec((tokens, width), lambda n: (0, 0))]
        + [pl.BlockSpec(memory_space=pl.ANY)] * len(before),
        out_specs=[weight, weight, pre, pre],
        out_shape=[
            jax.ShapeDtypeStruct((width, hidden), BF16),
            jax.ShapeDtypeStruct((width, hidden), BF16),
            jax.ShapeDtypeStruct((tokens, hidden // parts), F32),
            jax.ShapeDtypeStruct((tokens, hidden // parts), F32),
        ],
        input_output_aliases={5 + i: i for i in range(len(before))},
        compiler_params=params(),
        cost_estimate=cost(4 * tokens * width * hidden // parts, 8 * width * hidden // parts),
        name="mask_in",
    )(gate, up, gate_mask, up_mask, center, *before)


def mask_down_kernel(down_ref, mask_ref, query_ref, down_out, lam_ref):
    for k in range(down_ref.shape[0] // BLK):
        rows = slice(k * BLK, (k + 1) * BLK)
        down_out[rows, :] = down_ref[rows, :] * mask_ref[k : k + 1, :]

    @pl.when(pl.program_id(0) == 0)
    def _():
        lam_ref[...] = jnp.zeros_like(lam_ref)

    lam_ref[...] += lax.dot_general(
        query_ref[...], down_out[...], (((1,), (1,)), ((), ())), preferred_element_type=F32
    )


def mask_down(down, mask, query):
    hidden, width = down.shape
    tokens = query.shape[0]
    tile = 512
    return pl.pallas_call(
        mask_down_kernel,
        grid=(width // tile,),
        in_specs=[
            pl.BlockSpec((hidden, tile), lambda n: (0, n)),
            pl.BlockSpec((hidden // BLK, tile), lambda n: (0, n)),
            pl.BlockSpec((tokens, tile), lambda n: (0, n)),
        ],
        out_specs=[
            pl.BlockSpec((hidden, tile), lambda n: (0, n)),
            pl.BlockSpec((tokens, hidden), lambda n: (0, 0)),
        ],
        out_shape=[
            jax.ShapeDtypeStruct((hidden, width), BF16),
            jax.ShapeDtypeStruct((tokens, hidden), F32),
        ],
        compiler_params=params(),
        cost_estimate=cost(2 * tokens * width * hidden, 4 * width * hidden),
        name="mask_down",
    )(down, mask, query)


def gens_in_kernel(chunks, tok_ref, *refs):
    sides = (len(refs) - 6) // chunks
    parts = refs[: sides * chunks]
    gate_ref, up_ref, slope_ref, act_ref, out_ref, rows_ref = refs[sides * chunks :]
    lead, tokens, group, cols = parts[0].shape
    all_rows = lead * group
    slots = sides * MOST

    @pl.when(pl.program_id(0) == 0)
    def _():
        for s in range(slots):
            side = s // MOST
            tok = tok_ref[s]
            for c in range(chunks):
                for z in range(lead):
                    at = s * all_rows + z * group
                    rows_ref[at : at + group, c * cols : (c + 1) * cols] = parts[
                        side * chunks + c
                    ][z, tok]

    gate = jnp.dot(rows_ref[...], gate_ref[...], preferred_element_type=F32)
    up = jnp.dot(rows_ref[...], up_ref[...], preferred_element_type=F32)
    for s in range(slots):
        tok = tok_ref[s] + tokens * (s // MOST)
        here = slice(s * all_rows, (s + 1) * all_rows)
        out_ref[here, :] = (
            slope_ref[tok] * gate[here, :] + act_ref[tok] * up[here, :]
        ).astype(BF16)


def gens_in(tok, blocks, gate, up, slope, act):
    width, hidden = gate.shape
    chunks = len(blocks[0])
    sides = len(blocks)
    lead, tokens, group, _ = blocks[0][0].shape
    rows = sides * MOST * lead * group
    tile = min(256, hidden)
    part = pl.BlockSpec(
        blocks[0][0].shape, lambda n, t: (0, 0, 0, 0), pipeline_mode=pl.Buffered(1)
    )
    weight = pl.BlockSpec((width, tile), lambda n, t: (0, n))
    coef = pl.BlockSpec((sides * tokens, 1, tile), lambda n, t: (0, 0, n))
    return pl.pallas_call(
        functools.partial(gens_in_kernel, chunks),
        grid_spec=pltpu.PrefetchScalarGridSpec(
            num_scalar_prefetch=1,
            grid=(hidden // tile,),
            in_specs=[part] * (sides * chunks) + [weight, weight, coef, coef],
            out_specs=pl.BlockSpec((rows, tile), lambda n, t: (0, n)),
            scratch_shapes=[pltpu.VMEM((rows, width), BF16)],
        ),
        out_shape=jax.ShapeDtypeStruct((rows, hidden), BF16),
        compiler_params=params(),
        cost_estimate=cost(4 * rows * width * hidden, 4 * width * hidden + 2 * rows * width),
        name="gens_in",
    )(tok, *[p for block in blocks for p in block], gate, up, slope, act)


def gens_out_kernel(tok_ref, valid_ref, weight_ref, hidden_ref, down_ref, *out_refs):
    lead, _, group, _ = out_refs[0].shape
    all_rows = lead * group
    for out_ref in out_refs:
        out_ref[...] = jnp.zeros_like(out_ref)
    total = jnp.dot(hidden_ref[...], down_ref[...], preferred_element_type=F32)
    for s in range(len(out_refs) * MOST):
        out_ref = out_refs[s // MOST]

        @pl.when(valid_ref[s] > 0)
        def _():
            for z in range(lead):
                at = s * all_rows + z * group
                out_ref[z, tok_ref[s]] = (total[at : at + group, :] * weight_ref[s]).astype(BF16)


def gens_out(tok, valid, weight, hidden_gens, down, chunk, cols, lead, tokens, sides):
    rows, hidden = hidden_gens.shape
    group = rows // (sides * MOST * lead)
    tile = 512
    start = chunk * cols // tile
    return pl.pallas_call(
        gens_out_kernel,
        grid_spec=pltpu.PrefetchScalarGridSpec(
            num_scalar_prefetch=3,
            grid=(cols // tile,),
            in_specs=[
                pl.BlockSpec((rows, hidden), lambda n, *_: (0, 0), pipeline_mode=pl.Buffered(1)),
                pl.BlockSpec((hidden, tile), lambda n, *_: (0, start + n)),
            ],
            out_specs=[
                pl.BlockSpec((lead, tokens, group, tile), lambda n, *_: (0, 0, 0, n))
            ]
            * sides,
        ),
        out_shape=[jax.ShapeDtypeStruct((lead, tokens, group, cols), BF16)] * sides,
        compiler_params=params(),
        cost_estimate=cost(2 * rows * hidden * cols, 2 * hidden * cols + 4 * rows * cols),
        name="gens_out",
    )(tok, valid, weight, hidden_gens, down)


def shards(
    center, gens, query, routes, route_weights, gate_weight, up_weight, down_weight, block_mask
):
    experts = lax.axis_size("expert")
    tensors = lax.axis_size("tensor")
    tokens, rows_here, width = gens.shape
    me = lax.axis_index("expert")

    def across(value, distance):
        return lax.ppermute(value, "expert", [(i, i ^ distance) for i in range(experts)])

    pair = jnp.concatenate([center, query], axis=0)
    info = jnp.concatenate([routes.astype(F32), route_weights], axis=1)
    pairs = [pair] + [across(pair, r) for r in range(1, experts)]
    infos = jnp.stack([info] + [across(info, r) for r in range(1, experts)])
    center_all = jnp.concatenate([p[:tokens] for p in pairs], axis=0)
    query_all = jnp.concatenate([p[tokens:] for p in pairs], axis=0)

    aligned = rows_here % 16 == 0

    def back(value, distance):
        return lax.ppermute(
            value, "tensor", [(i, (i + distance) % tensors) for i in range(tensors)]
        )

    cols = width // CHUNKS_IN
    own, far = [], []
    for c in range(CHUNKS_IN):
        piece = gens[:, :, c * cols : (c + 1) * cols]
        if aligned:
            part = jnp.stack([piece] + [back(piece, d) for d in range(1, tensors)])
        else:
            part = lax.all_gather(piece, "tensor", axis=1, tiled=True)[None]
        own.append(part)
        far.append(across(part, 2))
    near = [across(p, 1) for p in own]
    far_near = [across(p, 1) for p in far]

    hit = (infos[:, :, :2] == me.astype(F32)).astype(F32)
    used = jnp.sum(hit, axis=2)
    token_weight = jnp.sum(hit * infos[:, :, 2:], axis=2)
    order = jnp.arange(tokens)
    earlier = (order[None, :] < order[:, None]).astype(F32)
    place = jnp.sum(used[:, None, :] * earlier[None], axis=2)
    slot = jnp.arange(MOST, dtype=F32)
    match = used[:, None, :] * (place[:, None, :] == slot[None, :, None]).astype(F32)
    tok = jnp.sum(match * jnp.arange(tokens, dtype=F32), axis=2).astype(jnp.int32).reshape(-1)
    valid = jnp.sum(match, axis=2).astype(jnp.int32).reshape(-1)
    slot_weight = jnp.sum(match * token_weight[:, None, :], axis=2).reshape(-1)

    mask = block_mask[0].astype(BF16)
    gate_mask = jnp.repeat(mask[0], BLK, axis=1)
    up_mask = jnp.repeat(mask[1], BLK, axis=1)
    down_mask = jnp.repeat(mask[2].T, BLK, axis=1)
    down, lam = mask_down(down_weight[0], down_mask, query_all)
    masked, pre = (), []
    parts = CHUNKS_IN - 1
    done = lam
    for i in range(parts):
        start, own[i] = lax.optimization_barrier((center_all, own[i], done))[:2]
        *masked, gate_pre, up_pre = mask_in(
            gate_weight[0], up_weight[0], gate_mask, up_mask, start, i, parts, masked
        )
        pre.append((gate_pre, up_pre))
        done = gate_pre
    gate, up = masked
    gate_center = jnp.concatenate([p[0] for p in pre], axis=1)
    up_center = jnp.concatenate([p[1] for p in pre], axis=1)
    gate_center, own[-1] = lax.optimization_barrier((gate_center, own[-1]))
    sigma = 1.0 / (1.0 + jnp.exp(-gate_center))
    act = gate_center * sigma
    slope = sigma * (1.0 + gate_center * (1.0 - sigma)) * up_center
    hidden_center = (act * up_center).astype(BF16)
    out_center = jnp.dot(hidden_center, down, preferred_element_type=F32)
    last = (((1,), (1,)), ((), ()))
    adjoint = lax.dot_general(
        (lam * slope).astype(BF16), gate, last, preferred_element_type=F32
    ) + lax.dot_general((lam * act).astype(BF16), up, last, preferred_element_type=F32)

    pair_out = jnp.stack([out_center, adjoint]) * token_weight.reshape(1, -1, 1)
    pair_out = pair_out.reshape(2, experts, tokens, width)
    lead = own[0].shape[0]
    hidden_gens = gens_in(
        tok, [own, near, far, far_near], gate, up, slope[:, None, :], act[:, None, :]
    )

    pair_out = after(pair_out, hidden_gens)
    pair_sum = pair_out[:, 0]
    for r in range(1, experts):
        pair_sum = pair_sum + across(pair_out[:, r], r)
    if aligned:
        mine = pair_sum
        for d in range(1, tensors):
            pair_sum = pair_sum + back(mine, d)
    else:
        pair_sum = lax.psum(pair_sum, "tensor")

    def add(*terms):
        return sum(t.astype(F32) for t in terms).astype(BF16)

    cols = width // CHUNKS_OUT
    outs, radii = [], []
    crossing, ordered = [], tok
    for c in range(CHUNKS_OUT):
        if c > 1:
            ordered = after(tok, crossing[c - 2][0])
        out = gens_out(
            ordered, valid, slot_weight, hidden_gens, down, c, cols, lead, tokens, experts
        )
        sent = add(out[2], across(out[3], 1))
        crossing.append((sent, add(out[0], across(out[1], 1))))
    for c in range(CHUNKS_OUT):
        sent, kept = crossing[c]
        block = add(kept, across(sent, 2))
        if aligned:
            token_gens = block[0].astype(F32)
            for d in range(1, tensors):
                token_gens = token_gens + back(block[d], tensors - d).astype(F32)
        else:
            block = block.reshape(tokens, tensors, rows_here, cols).transpose(1, 0, 2, 3)
            got = lax.all_to_all(block, "tensor", split_axis=0, concat_axis=0, tiled=True)
            token_gens = jnp.sum(got.astype(F32), axis=0)
        outs.append(token_gens.astype(BF16))
        radii.append(jnp.sum(jnp.abs(token_gens), axis=1))
    radius = jnp.concatenate(radii, axis=1)
    radius_part = radius.astype(BF16)
    if aligned:
        for d in range(1, tensors):
            radius = radius + back(radius_part, d).astype(F32)
    else:
        radius = lax.psum(radius_part, "tensor").astype(F32)
    return (
        pair_sum[0].astype(BF16),
        jnp.concatenate(outs, axis=2),
        radius,
        pair_sum[1],
    )


def solution(mesh):
    placed = (
        P(("groups", "expert"), None),
        P(("groups", "expert"), "tensor", None),
        P(("groups", "expert"), None),
        P(("groups", "expert"), None),
        P(("groups", "expert"), None),
        P("expert", None, "tensor"),
        P("expert", None, "tensor"),
        P("expert", "tensor", None),
        P("expert", None, None, "tensor"),
    )
    return jax.shard_map(
        shards,
        mesh=mesh,
        in_specs=placed,
        out_specs=(
            P(("groups", "expert"), None),
            P(("groups", "expert"), "tensor", None),
            P(("groups", "expert"), None),
            P(("groups", "expert"), None),
        ),
        check_vma=False,
    )
```

time: 821 us -> 360 us (0.44)
  waiting for transfers between devices: 459 us -> 82.9 us
  matrix products: 188 us -> 34.5 us
  Pallas kernels: 0 us -> 147 us
  local copies, waits for them, and re-layouts: 70.8 us -> 14.8 us
  starting transfers between devices: 19.3 us -> 69.3 us
  other arithmetic: 50.2 us -> 10.3 us
  blocking collectives: 17 us -> 0 us
  between operations: 14.9 us -> 1.28 us
    psum x1 -> x0, waiting for transfers between devices: 230 us -> none  [shards(): token_pair = lax.psum(pair_partial, 'tensor')]
    all_to_all x4 -> x0, waiting for transfers between devices: 229 us -> none  [the longest x1 203 us: shards(): lax.all_to_all(out_gens.reshape(all_rows, experts, MOST, width), 'expert'...]
    dot_general x10 -> x3, matrix products: 188 us -> 34.5 us  [the longest x1 12.3 us: shards(): lax.dot_general((lam * act).astype(BF16), up, last, preferred_element_typ...]
    pallas_call x0 -> x8, Pallas kernels: none -> 147 us  [the longest x1 50.3 us: gens_in(): pl.pallas_call(functools.partial(gens_in_kernel, chunks), grid_spec=pltpu...]
    ppermute x0 -> x57, waiting for transfers between devices: none -> 82.9 us  [the longest x27 45 us: back(): lax.ppermute(value, 'tensor', [(i, (i + distance) % tensors) for i in ran...]
    ppermute x0 -> x57, starting transfers between devices: none -> 69.3 us  [the longest x27 53.2 us: back(): lax.ppermute(value, 'tensor', [(i, (i + distance) % tensors) for i in ran...]
    mul x6 -> x0, local copies, waits for them, and re-layouts: 58.3 us -> none  [the longest x2 44.4 us: shards(): down_weight[0].reshape(hidden_blocks, BLK, width_blocks, BLK)]
    mul x1 -> x2, other arithmetic: 43 us -> 1.27 us  [the longest x1 1.21 us: shards(): pair_out = jnp.stack([out_center, adjoint]) * token_weight.reshape(1, -1, 1)]
  transfers between devices with their start and end apart: 6 -> 57, of which waited for: 3 -> 19; matrix products, arithmetic and copies ran while one was open for 32% -> 15% of each run, Pallas kernels for 0% -> 27%
where the time goes in v1:
time: 360 us
  Pallas kernels  147 us (41%)
  waiting for transfers between devices  82.9 us (23%)
  starting transfers between devices  69.3 us (19%)
  matrix products  34.5 us (10%)
  local copies, waits for them, and re-layouts  14.8 us (4%)
  other arithmetic  10.3 us (3%)
    ppermute x27, starting transfers between devices, back(): lax.ppermute(value, 'tensor', [(i, (i + distance) % tensors) for i in ran...  53.2 us
    pallas_call x1, Pallas kernels, gens_in(): pl.pallas_call(functools.partial(gens_in_kernel, chunks), grid_spec=pltpu...  50.3 us
    ppermute x27, waiting for transfers between devices, back(): lax.ppermute(value, 'tensor', [(i, (i + distance) % tensors) for i in ran...  45 us
    pallas_call x4, Pallas kernels, gens_out(): pl.pallas_call(gens_out_kernel, grid_spec=pltpu.PrefetchScalarGridSpec(nu...  41.1 us
    ppermute x30, waiting for transfers between devices, across(): lax.ppermute(value, 'expert', [(i, i ^ distance) for i in range(experts)])  37.8 us
    pallas_call x2, Pallas kernels, mask_in(): pl.pallas_call(mask_in_kernel, grid=(steps,), in_specs=[weight, weight, m...  34.9 us
    pallas_call x1, Pallas kernels, mask_down(): pl.pallas_call(mask_down_kernel, grid=(width // tile,), in_specs=[pl.Bloc...  20.2 us
    ppermute x30, starting transfers between devices, across(): lax.ppermute(value, 'expert', [(i, i ^ distance) for i in range(experts)])  16.2 us
  transfers between devices with their start and end apart: 57, of which 19 were waited for; matrix products, arithmetic and copies ran while one was open for 15% of the time, Pallas kernels for 27%

profile of v1, /device:TPU:0, one launch (start us, length us, event | category | flops | bytes accessed | tf_op | source)
XLA Modules:
  0.0 359.6 jit_solution(3914264918775961670)
XLA Ops:
  2.7 3.0 collective-permute-start.3
  5.7 2.6 collective-permute-start.4
  19.9 2.4 collective-permute-done.1
  24.8 2.8 collective-permute-start.11
  28.4 20.2 %mask_down.1 = (bf16[2048,6144]{1,0:T(8,128)(2,1)}, f32[16,2048]{1,0:T(8,128)}) custom-call(bf16[2048,6144]{1,0:T(8,128)(2,1)} %bitcast.132, bf16[16,6144]{1,0:T(8,128)(2,1)} %bitcast.135, bf16[16,6144]{1,0:T(8,128)(2,1)} %pad_maximum_fusion.5.query_ref), custom_call_target="tpu_custom_call" | custom-call | flops 20132660 | bytes 2516582 | tf_op jit(solution)/shard_map/mask_down/pallas_call | solution.py:91
  50.6 2.6 collective-permute-start.8
  56.6 3.4 collective-permute-done.6
  60.0 10.4 %collective-permute-done.7 = bf16[4,16,2048]{2,1,0:T(8,128)(2,1)S(1)} collective-permute-done((bf16[4,16,2048]{2,1,0:T(8,128)(2,1)}, bf16[4,16,2048]{2,1,0:T(8,128)(2,1)S(1)}, u32[]{:S(2)}, u32[]{:S(2)}) %collective-permute-start.7) | collective-permute-done | bytes 262176 | tf_op jit(solution)/shard_map/ppermute | solution.py:234
  72.1 17.4 %mask_in.2 = (bf16[6144,2048]{1,0:T(8,128)(2,1)}, bf16[6144,2048]{1,0:T(8,128)(2,1)}, f32[16,1024]{1,0:T(8,128)}, f32[16,1024]{1,0:T(8,128)}) custom-call(bf16[6144,2048]{1,0:T(8,128)(2,1)} %bitcast.128, bf16[6144,2048]{1,0:T(8,128)(2,1)} %bitcast.130, bf16[48,2048]{1,0:T(8,128)(2,1)} %get-tuple-element.120.gate_mask, ...), custom_call_target="tpu_custom_call" | custom-call | flops 20132660 | bytes 2516582 | tf_op jit(solution)/shard_map/mask_in/pallas_call | solution.py:54
  89.5 17.5 %mask_in.3 = (bf16[6144,2048]{1,0:T(8,128)(2,1)}, bf16[6144,2048]{1,0:T(8,128)(2,1)}, f32[16,1024]{1,0:T(8,128)}, f32[16,1024]{1,0:T(8,128)}) custom-call(bf16[6144,2048]{1,0:T(8,128)(2,1)} %bitcast.129, bf16[6144,2048]{1,0:T(8,128)(2,1)} %bitcast.131, bf16[48,2048]{1,0:T(8,128)(2,1)} %get-tuple-element.120.gate_mask, ...), custom_call_target="tpu_custom_call", output_to_operand_aliasing={{0}: (5, {}), {1}: (6, {})} | custom-call | flops 20132660 | bytes 2516582 | tf_op jit(solution)/shard_map/mask_in/pallas_call | solution.py:54
  110.4 10.7 %fusion.15 = f32[16,6144]{1,0:T(8,128)} fusion(bf16[2048,6144]{1,0:T(8,128)(2,1)} %get-tuple-element.49.down_ref, f32[16,2048]{1,0:T(8,128)S(1)} %constant_dynamic-update-slice_fusion, f32[16,2048]{1,0:T(8,128)S(1)} %pad_maximum_fusion.6), kind=kOutput, calls=%fused_computation.78 | convolution fusion | flops 402849792 | bytes 25821184 | tf_op jit(solution)/shard_map/dot_general | solution.py:286
  122.9 11.5 %fusion.16 = f32[16,6144]{1,0:T(8,128)S(1)} fusion(bf16[6144,2048]{1,0:T(8,128)(2,1)} %get-tuple-element.50.refs_12_, f32[16,2048]{1,0:T(8,128)S(1)} %copy-done.3, f32[16,2048]{1,0:T(8,128)S(1)} %constant_dynamic-update-slice_fusion, f32[16,2048]{1,0:T(8,128)S(1)} %pad_maximum_fusion.6), kind=kOutput, calls=%fused_computation.79 | convolution fusion | flops 402980864 | bytes 25952256 | tf_op jit(solution)/shard_map/dot_general | solution.py:288
  134.4 12.3 %convolution_add_fusion = f32[16,6144]{1,0:T(8,128)} fusion(f32[16,6144]{1,0:T(8,128)S(1)} %fusion.16, bf16[6144,2048]{1,0:T(8,128)(2,1)} %get-tuple-element.51.refs_13_, f32[16,2048]{1,0:T(8,128)S(1)} %copy-done.3, f32[16,2048]{1,0:T(8,128)S(1)} %pad_maximum_fusion.6), kind=kOutput, calls=%fused_computation | convolution fusion | flops 402948096 | bytes 26214400 | tf_op jit(solution)/shard_map/dot_general | solution.py:290
  156.3 50.3 %gens_in.1.hidden_ref = bf16[768,2048]{1,0:T(8,128)(2,1)} custom-call(s32[12]{0:T(128)} %convert_element_type.249.tok_ref, bf16[4,4,16,2048]{3,2,1,0:T(8,128)(2,1)} %copy-done, bf16[4,4,16,2048]{3,2,1,0:T(8,128)(2,1)} %copy-done.2, bf16[4,4,16,2048]{3,2,1,0:T(8,128)(2,1)} %copy-done.1, bf16[4,4,16,2048]{3,2,1,0:T(8,128)(2,1)} %collective-permute-done.15.refs_3_, ...), custom_call_target="tpu_custom_call" | custom-call | flops 1932735232 | bytes 2988441 | tf_op jit(solution)/shard_map/gens_in/pallas_call | solution.py:155
  208.5 6.1 %collective-permute-done.25 = f32[2,4,6144]{2,1,0:T(4,128)S(1)} collective-permute-done((f32[2,4,6144]{2,1,0:T(4,128)S(1)}, f32[2,4,6144]{2,1,0:T(4,128)S(1)}, u32[]{:S(2)}, u32[]{:S(2)}) %collective-permute-start.25) | collective-permute-done | bytes 196640 | tf_op jit(solution)/shard_map/ppermute | solution.py:222
  214.6 2.9 collective-permute-done.26
  217.7 7.2 %collective-permute-start.29 = (f32[2,4,6144]{2,1,0:T(4,128)S(1)}, f32[2,4,6144]{2,1,0:T(4,128)S(1)}, u32[]{:S(2)}, u32[]{:S(2)}) collective-permute-start(f32[2,4,6144]{2,1,0:T(4,128)S(1)} %fusion.9), channel_id=1, source_target_pairs={{0,12},{4,0},{8,4},{12,8},{1,13},{5,1},{9,5},{13,9},{2,14},{6,2},{... | collective-permute-start | bytes 589832 | tf_op jit(solution)/shard_map/ppermute | solution.py:234
  226.9 10.3 %gens_out.4 = (bf16[4,4,16,1536]{3,2,1,0:T(8,128)(2,1)}, bf16[4,4,16,1536]{3,2,1,0:T(8,128)(2,1)}, bf16[4,4,16,1536]{3,2,1,0:T(8,128)(2,1)}, bf16[4,4,16,1536]{3,2,1,0:T(8,128)(2,1)}) custom-call(s32[12]{0:T(128)} %convert_element_type.249.tok_ref, s32[12]{0:T(128)} %convert_element_type.252.valid_ref, f32[12]{0:T(128)} %reshape.70.weight_ref, ...), custom_call_target="tpu_custom_call" | custom-call | flops 241591904 | bytes 550502 | tf_op jit(solution)/shard_map/gens_out/pallas_call | solution.py:192
  237.7 10.2 %gens_out.5 = (bf16[4,4,16,1536]{3,2,1,0:T(8,128)(2,1)}, bf16[4,4,16,1536]{3,2,1,0:T(8,128)(2,1)}, bf16[4,4,16,1536]{3,2,1,0:T(8,128)(2,1)}, bf16[4,4,16,1536]{3,2,1,0:T(8,128)(2,1)}) custom-call(s32[12]{0:T(128)} %convert_element_type.249.tok_ref, s32[12]{0:T(128)} %convert_element_type.252.valid_ref, f32[12]{0:T(128)} %reshape.70.weight_ref, ...), custom_call_target="tpu_custom_call" | custom-call | flops 241591904 | bytes 550502 | tf_op jit(solution)/shard_map/gens_out/pallas_call | solution.py:192
  252.5 10.3 %gens_out.6 = (bf16[4,4,16,1536]{3,2,1,0:T(8,128)(2,1)}, bf16[4,4,16,1536]{3,2,1,0:T(8,128)(2,1)}, bf16[4,4,16,1536]{3,2,1,0:T(8,128)(2,1)}, bf16[4,4,16,1536]{3,2,1,0:T(8,128)(2,1)}) custom-call(s32[12]{0:T(128)} %convert_element_type.249.tok_ref, s32[12]{0:T(128)} %convert_element_type.252.valid_ref, f32[12]{0:T(128)} %reshape.70.weight_ref, ...), custom_call_target="tpu_custom_call" | custom-call | flops 241591904 | bytes 550502 | tf_op jit(solution)/shard_map/gens_out/pallas_call | solution.py:192
  262.9 10.4 %gens_out.7 = (bf16[4,4,16,1536]{3,2,1,0:T(8,128)(2,1)}, bf16[4,4,16,1536]{3,2,1,0:T(8,128)(2,1)}, bf16[4,4,16,1536]{3,2,1,0:T(8,128)(2,1)}, bf16[4,4,16,1536]{3,2,1,0:T(8,128)(2,1)}) custom-call(s32[12]{0:T(128)} %convert_element_type.249.tok_ref, s32[12]{0:T(128)} %convert_element_type.252.valid_ref, f32[12]{0:T(128)} %reshape.70.weight_ref, ...), custom_call_target="tpu_custom_call" | custom-call | flops 241591904 | bytes 550502 | tf_op jit(solution)/shard_map/gens_out/pallas_call | solution.py:192
  274.3 4.0 %collective-permute-start.33 = (bf16[4,16,1536]{2,1,0:T(8,128)(2,1)S(1)}, bf16[4,16,1536]{2,1,0:T(8,128)(2,1)S(1)}, u32[]{:S(2)}, u32[]{:S(2)}) collective-permute-start(bf16[4,16,1536]{2,1,0:T(8,128)(2,1)S(1)} %get-tuple-element.87), channel_id=1, source_target_pairs={{0,12},{4,0},{8,4},{12,8},{1,13},{5,1},{9,5},{13,9},{2,14},{6,2},{... | collective-permute-start | bytes 589832 | tf_op jit(solution)/shard_map/ppermute | solution.py:234
  281.5 4.4 %collective-permute-done.38 = bf16[4,4,16,1536]{3,2,1,0:T(8,128)(2,1)S(1)} collective-permute-done((bf16[4,4,16,1536]{3,2,1,0:T(8,128)(2,1)S(1)}, bf16[4,4,16,1536]{3,2,1,0:T(8,128)(2,1)S(1)}, u32[]{:S(2)}, u32[]{:S(2)}) %collective-permute-start.38) | collective-permute-done | bytes 786464 | tf_op jit(solution)/shard_map/ppermute | solution.py:222
  287.0 3.8 %collective-permute-start.39 = (bf16[4,16,1536]{2,1,0:T(8,128)(2,1)S(1)}, bf16[4,16,1536]{2,1,0:T(8,128)(2,1)S(1)}, u32[]{:S(2)}, u32[]{:S(2)}) collective-permute-start(bf16[4,16,1536]{2,1,0:T(8,128)(2,1)S(1)} %get-tuple-element.90), channel_id=1, source_target_pairs={{0,12},{4,0},{8,4},{12,8},{1,13},{5,1},{9,5},{13,9},{2,14},{6,2},{... | collective-permute-start | bytes 589832 | tf_op jit(solution)/shard_map/ppermute | solution.py:234
  290.8 6.7 %collective-permute-done.34 = bf16[4,16,1536]{2,1,0:T(8,128)(2,1)S(1)} collective-permute-done((bf16[4,16,1536]{2,1,0:T(8,128)(2,1)S(1)}, bf16[4,16,1536]{2,1,0:T(8,128)(2,1)S(1)}, u32[]{:S(2)}, u32[]{:S(2)}) %collective-permute-start.34) | collective-permute-done | bytes 196640 | tf_op jit(solution)/shard_map/ppermute | solution.py:234
  297.5 8.0 %collective-permute-start.41 = (bf16[4,16,1536]{2,1,0:T(8,128)(2,1)S(1)}, bf16[4,16,1536]{2,1,0:T(8,128)(2,1)S(1)}, u32[]{:S(2)}, u32[]{:S(2)}) collective-permute-start(bf16[4,16,1536]{2,1,0:T(8,128)(2,1)S(1)} %get-tuple-element.91), channel_id=1, source_target_pairs={{0,4},{4,8},{8,12},{12,0},{1,5},{5,9},{9,13},{13,1},{2,6},{6,10},{... | collective-permute-start | bytes 589832 | tf_op jit(solution)/shard_map/ppermute | solution.py:234
  305.7 7.8 %collective-permute-done.40 = bf16[4,16,1536]{2,1,0:T(8,128)(2,1)S(1)} collective-permute-done((bf16[4,16,1536]{2,1,0:T(8,128)(2,1)S(1)}, bf16[4,16,1536]{2,1,0:T(8,128)(2,1)S(1)}, u32[]{:S(2)}, u32[]{:S(2)}) %collective-permute-start.40) | collective-permute-done | bytes 196640 | tf_op jit(solution)/shard_map/ppermute | solution.py:234
  314.9 2.4 collective-permute-start.45
  318.5 14.0 %collective-permute-done.50 = bf16[4,4,16,1536]{3,2,1,0:T(8,128)(2,1)S(1)} collective-permute-done((bf16[4,4,16,1536]{3,2,1,0:T(8,128)(2,1)S(1)}, bf16[4,4,16,1536]{3,2,1,0:T(8,128)(2,1)S(1)}, u32[]{:S(2)}, u32[]{:S(2)}) %collective-permute-start.50) | collective-permute-done | bytes 786464 | tf_op jit(solution)/shard_map/ppermute | solution.py:222
  335.1 3.5 collective-permute-done.51
  338.6 12.4 %collective-permute-done.52 = bf16[4,16,1536]{2,1,0:T(8,128)(2,1)S(1)} collective-permute-done((bf16[4,16,1536]{2,1,0:T(8,128)(2,1)S(1)}, bf16[4,16,1536]{2,1,0:T(8,128)(2,1)S(1)}, u32[]{:S(2)}, u32[]{:S(2)}) %collective-permute-start.52) | collective-permute-done | bytes 196640 | tf_op jit(solution)/shard_map/ppermute | solution.py:234
  354.3 2.8 collective-permute-start.56
  (216 shorter events, 64.1 us)
Async XLA Ops:
  2.7 22.1 %collective-permute-start.3 = (bf16[4,16,2048]{2,1,0:T(8,128)(2,1)S(1)}, bf16[4,16,2048]{2,1,0:T(8,128)(2,1)S(1)}, u32[]{:S(2)}, u32[]{:S(2)}) collective-permute-start(bf16[4,16,2048]{2,1,0:T(8,128)(2,1)S(1)} %get-tuple-element.105), channel_id=1, source_target_pairs={{0,4},{4,8},{8,12},{12,0},{1,5},{5,9},{9,13},{13,1},{2,6},{6,10},{... | collective-permute-start | bytes 786440 | tf_op jit(solution)/shard_map/ppermute | solution.py:234
  5.7 42.9 %collective-permute-start.4 = (bf16[4,16,2048]{2,1,0:T(8,128)(2,1)S(1)}, bf16[4,16,2048]{2,1,0:T(8,128)(2,1)S(1)}, u32[]{:S(2)}, u32[]{:S(2)}) collective-permute-start(bf16[4,16,2048]{2,1,0:T(8,128)(2,1)S(1)} %get-tuple-element.105), channel_id=1, source_target_pairs={{0,8},{4,12},{8,0},{12,4},{1,9},{5,13},{9,1},{13,5},{2,10},{6,14},... | collective-permute-start | bytes 786440 | tf_op jit(solution)/shard_map/ppermute | solution.py:234
  8.3 40.4 %collective-permute-start.5 = (bf16[4,16,2048]{2,1,0:T(8,128)(2,1)S(1)}, bf16[4,16,2048]{2,1,0:T(8,128)(2,1)S(1)}, u32[]{:S(2)}, u32[]{:S(2)}) collective-permute-start(bf16[4,16,2048]{2,1,0:T(8,128)(2,1)S(1)} %get-tuple-element.105), channel_id=1, source_target_pairs={{0,12},{4,0},{8,4},{12,8},{1,13},{5,1},{9,5},{13,9},{2,14},{6,2},{... | collective-permute-start | bytes 786440 | tf_op jit(solution)/shard_map/ppermute | solution.py:234
  22.3 28.3 %collective-permute-start.9 = (bf16[4,16,2048]{2,1,0:T(8,128)(2,1)S(1)}, bf16[4,16,2048]{2,1,0:T(8,128)(2,1)S(1)}, u32[]{:S(2)}, u32[]{:S(2)}) collective-permute-start(bf16[4,16,2048]{2,1,0:T(8,128)(2,1)S(1)} %get-tuple-element.106), channel_id=1, source_target_pairs={{0,4},{4,8},{8,12},{12,0},{1,5},{5,9},{9,13},{13,1},{2,6},{6,10},{... | collective-permute-start | bytes 786440 | tf_op jit(solution)/shard_map/ppermute | solution.py:234
  23.7 30.6 %collective-permute-start.10 = (bf16[4,16,2048]{2,1,0:T(8,128)(2,1)S(1)}, bf16[4,16,2048]{2,1,0:T(8,128)(2,1)S(1)}, u32[]{:S(2)}, u32[]{:S(2)}) collective-permute-start(bf16[4,16,2048]{2,1,0:T(8,128)(2,1)S(1)} %get-tuple-element.106), channel_id=1, source_target_pairs={{0,8},{4,12},{8,0},{12,4},{1,9},{5,13},{9,1},{13,5},{2,10},{6,14},... | collective-permute-start | bytes 786440 | tf_op jit(solution)/shard_map/ppermute | solution.py:234
  24.8 30.3 %collective-permute-start.11 = (bf16[4,16,2048]{2,1,0:T(8,128)(2,1)S(1)}, bf16[4,16,2048]{2,1,0:T(8,128)(2,1)S(1)}, u32[]{:S(2)}, u32[]{:S(2)}) collective-permute-start(bf16[4,16,2048]{2,1,0:T(8,128)(2,1)S(1)} %get-tuple-element.106), channel_id=1, source_target_pairs={{0,12},{4,0},{8,4},{12,8},{1,13},{5,1},{9,5},{13,9},{2,14},{6,2},{... | collective-permute-start | bytes 786440 | tf_op jit(solution)/shard_map/ppermute | solution.py:234
  48.8 21.6 %collective-permute-start.7 = (bf16[4,16,2048]{2,1,0:T(8,128)(2,1)}, bf16[4,16,2048]{2,1,0:T(8,128)(2,1)S(1)}, u32[]{:S(2)}, u32[]{:S(2)}) collective-permute-start(bf16[4,16,2048]{2,1,0:T(8,128)(2,1)} %get-tuple-element.107), channel_id=1, source_target_pairs={{0,8},{4,12},{8,0},{12,4},{1,9},{5,13},{9,1},{13,5},{2,10},{6,14},... | collective-permute-start | bytes 786440 | tf_op jit(solution)/shard_map/ppermute | solution.py:234
  50.6 19.8 %collective-permute-start.8 = (bf16[4,16,2048]{2,1,0:T(8,128)(2,1)}, bf16[4,16,2048]{2,1,0:T(8,128)(2,1)S(1)}, u32[]{:S(2)}, u32[]{:S(2)}) collective-permute-start(bf16[4,16,2048]{2,1,0:T(8,128)(2,1)} %get-tuple-element.107), channel_id=1, source_target_pairs={{0,12},{4,0},{8,4},{12,8},{1,13},{5,1},{9,5},{13,9},{2,14},{6,2},{... | collective-permute-start | bytes 786440 | tf_op jit(solution)/shard_map/ppermute | solution.py:234
  54.3 93.9 %collective-permute-start.18 = (bf16[4,4,16,2048]{3,2,1,0:T(8,128)(2,1)S(1)}, bf16[4,4,16,2048]{3,2,1,0:T(8,128)(2,1)}, u32[]{:S(2)}, u32[]{:S(2)}) collective-permute-start(bf16[4,4,16,2048]{3,2,1,0:T(8,128)(2,1)S(1)} %pad_maximum_fusion.refs_0_), channel_id=1, source_target_pairs={{0,2},{1,3},{2,0},{3,1},{4,6},{5,7},{6,4},{7,5},{8,10},{9,11},{10,... | collective-permute-start | bytes 3145736 | tf_op jit(solution)/shard_map/ppermute | solution.py:222
  55.3 92.6 %collective-permute-start.20 = (bf16[4,4,16,2048]{3,2,1,0:T(8,128)(2,1)S(1)}, bf16[4,4,16,2048]{3,2,1,0:T(8,128)(2,1)}, u32[]{:S(2)}, u32[]{:S(2)}) collective-permute-start(bf16[4,4,16,2048]{3,2,1,0:T(8,128)(2,1)S(1)} %pad_maximum_fusion.2.refs_2_), channel_id=1, source_target_pairs={{0,2},{1,3},{2,0},{3,1},{4,6},{5,7},{6,4},{7,5},{8,10},{9,11},{10,... | collective-permute-start | bytes 3145736 | tf_op jit(solution)/shard_map/ppermute | solution.py:222
  60.0 88.7 %collective-permute-start.17 = (bf16[4,4,16,2048]{3,2,1,0:T(8,128)(2,1)S(1)}, bf16[4,4,16,2048]{3,2,1,0:T(8,128)(2,1)}, u32[]{:S(2)}, u32[]{:S(2)}) collective-permute-start(bf16[4,4,16,2048]{3,2,1,0:T(8,128)(2,1)S(1)} %pad_maximum_fusion.2.refs_2_), channel_id=1, source_target_pairs={{0,1},{1,0},{2,3},{3,2},{4,5},{5,4},{6,7},{7,6},{8,9},{9,8},{10,11... | collective-permute-start | bytes 3145736 | tf_op jit(solution)/shard_map/ppermute | solution.py:222
  70.4 79.8 %collective-permute-start.15 = (bf16[4,4,16,2048]{3,2,1,0:T(8,128)(2,1)S(1)}, bf16[4,4,16,2048]{3,2,1,0:T(8,128)(2,1)}, u32[]{:S(2)}, u32[]{:S(2)}) collective-permute-start(bf16[4,4,16,2048]{3,2,1,0:T(8,128)(2,1)S(1)} %pad_maximum_fusion.refs_0_), channel_id=1, source_target_pairs={{0,1},{1,0},{2,3},{3,2},{4,5},{5,4},{6,7},{7,6},{8,9},{9,8},{10,11... | collective-permute-start | bytes 3145736 | tf_op jit(solution)/shard_map/ppermute | solution.py:222
  70.6 77.9 %collective-permute-start.19 = (bf16[4,4,16,2048]{3,2,1,0:T(8,128)(2,1)S(1)}, bf16[4,4,16,2048]{3,2,1,0:T(8,128)(2,1)}, u32[]{:S(2)}, u32[]{:S(2)}) collective-permute-start(bf16[4,4,16,2048]{3,2,1,0:T(8,128)(2,1)S(1)} %pad_maximum_fusion.1.refs_1_), channel_id=1, source_target_pairs={{0,2},{1,3},{2,0},{3,1},{4,6},{5,7},{6,4},{7,5},{8,10},{9,11},{10,... | collective-permute-start | bytes 3145736 | tf_op jit(solution)/shard_map/ppermute | solution.py:222
  217.7 30.3 %collective-permute-start.29 = (f32[2,4,6144]{2,1,0:T(4,128)S(1)}, f32[2,4,6144]{2,1,0:T(4,128)S(1)}, u32[]{:S(2)}, u32[]{:S(2)}) collective-permute-start(f32[2,4,6144]{2,1,0:T(4,128)S(1)} %fusion.9), channel_id=1, source_target_pairs={{0,12},{4,0},{8,4},{12,8},{1,13},{5,1},{9,5},{13,9},{2,14},{6,2},{... | collective-permute-start | bytes 589832 | tf_op jit(solution)/shard_map/ppermute | solution.py:234
  224.9 23.1 %collective-permute-start.28 = (f32[2,4,6144]{2,1,0:T(4,128)S(1)}, f32[2,4,6144]{2,1,0:T(4,128)S(1)}, u32[]{:S(2)}, u32[]{:S(2)}) collective-permute-start(f32[2,4,6144]{2,1,0:T(4,128)S(1)} %fusion.9), channel_id=1, source_target_pairs={{0,8},{4,12},{8,0},{12,4},{1,9},{5,13},{9,1},{13,5},{2,10},{6,14},... | collective-permute-start | bytes 589832 | tf_op jit(solution)/shard_map/ppermute | solution.py:234
  225.4 23.1 %collective-permute-start.27 = (f32[2,4,6144]{2,1,0:T(4,128)S(1)}, f32[2,4,6144]{2,1,0:T(4,128)S(1)}, u32[]{:S(2)}, u32[]{:S(2)}) collective-permute-start(f32[2,4,6144]{2,1,0:T(4,128)S(1)} %fusion.9), channel_id=1, source_target_pairs={{0,4},{4,8},{8,12},{12,0},{1,5},{5,9},{9,13},{13,1},{2,6},{6,10},{... | collective-permute-start | bytes 589832 | tf_op jit(solution)/shard_map/ppermute | solution.py:234
  237.2 36.1 %collective-permute-start.30 = (bf16[4,4,16,1536]{3,2,1,0:T(8,128)(2,1)}, bf16[4,4,16,1536]{3,2,1,0:T(8,128)(2,1)S(1)}, u32[]{:S(2)}, u32[]{:S(2)}) collective-permute-start(bf16[4,4,16,1536]{3,2,1,0:T(8,128)(2,1)} %get-tuple-element.57), channel_id=1, source_target_pairs={{0,1},{1,0},{2,3},{3,2},{4,5},{5,4},{6,7},{7,6},{8,9},{9,8},{10,11... | collective-permute-start | bytes 2359304 | tf_op jit(solution)/shard_map/ppermute | solution.py:222
  248.0 31.5 %collective-permute-start.36 = (bf16[4,4,16,1536]{3,2,1,0:T(8,128)(2,1)}, bf16[4,4,16,1536]{3,2,1,0:T(8,128)(2,1)S(1)}, u32[]{:S(2)}, u32[]{:S(2)}) collective-permute-start(bf16[4,4,16,1536]{3,2,1,0:T(8,128)(2,1)} %get-tuple-element.61), channel_id=1, source_target_pairs={{0,1},{1,0},{2,3},{3,2},{4,5},{5,4},{6,7},{7,6},{8,9},{9,8},{10,11... | collective-permute-start | bytes 2359304 | tf_op jit(solution)/shard_map/ppermute | solution.py:222
  249.5 24.2 %collective-permute-start.32 = (bf16[4,4,16,1536]{3,2,1,0:T(8,128)(2,1)S(1)}, bf16[4,4,16,1536]{3,2,1,0:T(8,128)(2,1)S(1)}, u32[]{:S(2)}, u32[]{:S(2)}) collective-permute-start(bf16[4,4,16,1536]{3,2,1,0:T(8,128)(2,1)S(1)} %add_convert_fusion.10), channel_id=1, source_target_pairs={{0,2},{1,3},{2,0},{3,1},{4,6},{5,7},{6,4},{7,5},{8,10},{9,11},{10,... | collective-permute-start | bytes 2359304 | tf_op jit(solution)/shard_map/ppermute | solution.py:222
  251.1 34.8 %collective-permute-start.38 = (bf16[4,4,16,1536]{3,2,1,0:T(8,128)(2,1)S(1)}, bf16[4,4,16,1536]{3,2,1,0:T(8,128)(2,1)S(1)}, u32[]{:S(2)}, u32[]{:S(2)}) collective-permute-start(bf16[4,4,16,1536]{3,2,1,0:T(8,128)(2,1)S(1)} %add_convert_fusion.7), channel_id=1, source_target_pairs={{0,2},{1,3},{2,0},{3,1},{4,6},{5,7},{6,4},{7,5},{8,10},{9,11},{10,... | collective-permute-start | bytes 2359304 | tf_op jit(solution)/shard_map/ppermute | solution.py:222
  273.3 41.2 %collective-permute-start.42 = (bf16[4,4,16,1536]{3,2,1,0:T(8,128)(2,1)S(1)}, bf16[4,4,16,1536]{3,2,1,0:T(8,128)(2,1)S(1)}, u32[]{:S(2)}, u32[]{:S(2)}) collective-permute-start(bf16[4,4,16,1536]{3,2,1,0:T(8,128)(2,1)S(1)} %copy-done.25), channel_id=1, source_target_pairs={{0,1},{1,0},{2,3},{3,2},{4,5},{5,4},{6,7},{7,6},{8,9},{9,8},{10,11... | collective-permute-start | bytes 2359304 | tf_op jit(solution)/shard_map/ppermute | solution.py:222
  278.5 18.9 %collective-permute-start.34 = (bf16[4,16,1536]{2,1,0:T(8,128)(2,1)S(1)}, bf16[4,16,1536]{2,1,0:T(8,128)(2,1)S(1)}, u32[]{:S(2)}, u32[]{:S(2)}) collective-permute-start(bf16[4,16,1536]{2,1,0:T(8,128)(2,1)S(1)} %get-tuple-element.89), channel_id=1, source_target_pairs={{0,8},{4,12},{8,0},{12,4},{1,9},{5,13},{9,1},{13,5},{2,10},{6,14},... | collective-permute-start | bytes 589832 | tf_op jit(solution)/shard_map/ppermute | solution.py:234
  279.5 18.0 %collective-permute-start.35 = (bf16[4,16,1536]{2,1,0:T(8,128)(2,1)S(1)}, bf16[4,16,1536]{2,1,0:T(8,128)(2,1)S(1)}, u32[]{:S(2)}, u32[]{:S(2)}) collective-permute-start(bf16[4,16,1536]{2,1,0:T(8,128)(2,1)S(1)} %get-tuple-element.88), channel_id=1, source_target_pairs={{0,4},{4,8},{8,12},{12,0},{1,5},{5,9},{9,13},{13,1},{2,6},{6,10},{... | collective-permute-start | bytes 589832 | tf_op jit(solution)/shard_map/ppermute | solution.py:234
  285.9 28.5 %collective-permute-start.44 = (bf16[4,4,16,1536]{3,2,1,0:T(8,128)(2,1)S(1)}, bf16[4,4,16,1536]{3,2,1,0:T(8,128)(2,1)S(1)}, u32[]{:S(2)}, u32[]{:S(2)}) collective-permute-start(bf16[4,4,16,1536]{3,2,1,0:T(8,128)(2,1)S(1)} %add_convert_fusion.4), channel_id=1, source_target_pairs={{0,2},{1,3},{2,0},{3,1},{4,6},{5,7},{6,4},{7,5},{8,10},{9,11},{10,... | collective-permute-start | bytes 2359304 | tf_op jit(solution)/shard_map/ppermute | solution.py:222
  287.0 18.6 %collective-permute-start.39 = (bf16[4,16,1536]{2,1,0:T(8,128)(2,1)S(1)}, bf16[4,16,1536]{2,1,0:T(8,128)(2,1)S(1)}, u32[]{:S(2)}, u32[]{:S(2)}) collective-permute-start(bf16[4,16,1536]{2,1,0:T(8,128)(2,1)S(1)} %get-tuple-element.90), channel_id=1, source_target_pairs={{0,12},{4,0},{8,4},{12,8},{1,13},{5,1},{9,5},{13,9},{2,14},{6,2},{... | collective-permute-start | bytes 589832 | tf_op jit(solution)/shard_map/ppermute | solution.py:234
  297.5 16.8 %collective-permute-start.41 = (bf16[4,16,1536]{2,1,0:T(8,128)(2,1)S(1)}, bf16[4,16,1536]{2,1,0:T(8,128)(2,1)S(1)}, u32[]{:S(2)}, u32[]{:S(2)}) collective-permute-start(bf16[4,16,1536]{2,1,0:T(8,128)(2,1)S(1)} %get-tuple-element.91), channel_id=1, source_target_pairs={{0,4},{4,8},{8,12},{12,0},{1,5},{5,9},{9,13},{13,1},{2,6},{6,10},{... | collective-permute-start | bytes 589832 | tf_op jit(solution)/shard_map/ppermute | solution.py:234
  313.5 18.9 %collective-permute-start.50 = (bf16[4,4,16,1536]{3,2,1,0:T(8,128)(2,1)S(1)}, bf16[4,4,16,1536]{3,2,1,0:T(8,128)(2,1)S(1)}, u32[]{:S(2)}, u32[]{:S(2)}) collective-permute-start(bf16[4,4,16,1536]{3,2,1,0:T(8,128)(2,1)S(1)} %add_convert_fusion.1), channel_id=1, source_target_pairs={{0,2},{1,3},{2,0},{3,1},{4,6},{5,7},{6,4},{7,5},{8,10},{9,11},{10,... | collective-permute-start | bytes 2359304 | tf_op jit(solution)/shard_map/ppermute | solution.py:222
  314.9 18.1 %collective-permute-start.45 = (bf16[4,16,1536]{2,1,0:T(8,128)(2,1)S(1)}, bf16[4,16,1536]{2,1,0:T(8,128)(2,1)S(1)}, u32[]{:S(2)}, u32[]{:S(2)}) collective-permute-start(bf16[4,16,1536]{2,1,0:T(8,128)(2,1)S(1)} %get-tuple-element.93), channel_id=1, source_target_pairs={{0,12},{4,0},{8,4},{12,8},{1,13},{5,1},{9,5},{13,9},{2,14},{6,2},{... | collective-permute-start | bytes 589832 | tf_op jit(solution)/shard_map/ppermute | solution.py:234
  317.3 17.6 %collective-permute-start.46 = (bf16[4,16,1536]{2,1,0:T(8,128)(2,1)S(1)}, bf16[4,16,1536]{2,1,0:T(8,128)(2,1)S(1)}, u32[]{:S(2)}, u32[]{:S(2)}) collective-permute-start(bf16[4,16,1536]{2,1,0:T(8,128)(2,1)S(1)} %get-tuple-element.95), channel_id=1, source_target_pairs={{0,8},{4,12},{8,0},{12,4},{1,9},{5,13},{9,1},{13,5},{2,10},{6,14},... | collective-permute-start | bytes 589832 | tf_op jit(solution)/shard_map/ppermute | solution.py:234
  317.3 17.6 %collective-permute-start.47 = (bf16[4,16,1536]{2,1,0:T(8,128)(2,1)S(1)}, bf16[4,16,1536]{2,1,0:T(8,128)(2,1)S(1)}, u32[]{:S(2)}, u32[]{:S(2)}) collective-permute-start(bf16[4,16,1536]{2,1,0:T(8,128)(2,1)S(1)} %get-tuple-element.94), channel_id=1, source_target_pairs={{0,4},{4,8},{8,12},{12,0},{1,5},{5,9},{9,13},{13,1},{2,6},{6,10},{... | collective-permute-start | bytes 589832 | tf_op jit(solution)/shard_map/ppermute | solution.py:234
  332.9 18.1 %collective-permute-start.52 = (bf16[4,16,1536]{2,1,0:T(8,128)(2,1)S(1)}, bf16[4,16,1536]{2,1,0:T(8,128)(2,1)S(1)}, u32[]{:S(2)}, u32[]{:S(2)}) collective-permute-start(bf16[4,16,1536]{2,1,0:T(8,128)(2,1)S(1)} %get-tuple-element.98), channel_id=1, source_target_pairs={{0,8},{4,12},{8,0},{12,4},{1,9},{5,13},{9,1},{13,5},{2,10},{6,14},... | collective-permute-start | bytes 589832 | tf_op jit(solution)/shard_map/ppermute | solution.py:234
  333.0 18.0 %collective-permute-start.53 = (bf16[4,16,1536]{2,1,0:T(8,128)(2,1)S(1)}, bf16[4,16,1536]{2,1,0:T(8,128)(2,1)S(1)}, u32[]{:S(2)}, u32[]{:S(2)}) collective-permute-start(bf16[4,16,1536]{2,1,0:T(8,128)(2,1)S(1)} %get-tuple-element.97), channel_id=1, source_target_pairs={{0,4},{4,8},{8,12},{12,0},{1,5},{5,9},{9,13},{13,1},{2,6},{6,10},{... | collective-permute-start | bytes 589832 | tf_op jit(solution)/shard_map/ppermute | solution.py:234
  (51 other events, 523.4 us)
